TPU v7x, 256 devices: a whole 4x4x8 slice. The times are simulated.
256 devices in a mesh: row: 8 (over z), slab: 16 (over x, y), rep: 2 (over core).
Axes of the slice: x: 4, y: 4, z: 8, core: 2. Of those that a mesh axis runs over, the one named last changes fastest.
Arguments:
- t2_stored: float32 [4096, 40960], P('row', ('slab', 'rep')), may hold values from -6 to 6
- v_slab: float32 [1536, 40960], P('rep', 'slab'), may hold values from -0.03125 to 0.03125
- block_source: int32 [320], replicated, may hold values from 0 to 319, as said below
- r_in: float32 [4096, 1536], P(('row', 'slab'), 'rep'), may hold values from -6 to 6
Outputs:
- r_out: float32 [4096, 1536], P(('row', 'slab'), 'rep')
Inputs may be any that keep to these rules, and one draw needn't show every extreme that they name: block_source is a permutation of the 320 stored blocks. Slab index t owns the blocks k with k // 20 == t; stored block q lies on the device of slab and rep numbered q // 10. Every such device stores either none or exactly 2 blocks owned by any one slab index, and the slab indices it stores blocks for form a run of 5 consecutive indices counted modulo the slab axis.
All inputs are finite; a program needn't handle non-finite values.
Results may differ from a plain program's by a relative error of at most 0.000084.
Values sent between devices are 32-bit elements; how exact they have to be, the bound alone decides.
A program may use at most 128 MiB of HBM per device.

v0:
```python
import jax
import jax.numpy as jnp
from jax import lax
from jax.sharding import PartitionSpec as P

BLK = 128


def block_maps(block_source, nblk_total, stored, blk_dev):
    indices = jnp.arange(nblk_total, dtype=jnp.int32)
    matches = block_source[None, :] == indices[:, None]
    position = jnp.sum(jnp.where(matches, indices[None, :], 0), axis=1)
    owner = position // blk_dev
    holder = indices // stored
    earlier = (
        (holder[None, :] == holder[:, None])
        & (owner[None, :] == owner[:, None])
        & (indices[None, :] < indices[:, None])
    )
    slot_rank = jnp.sum(earlier.astype(jnp.int32), axis=1)
    return (owner, slot_rank)


def per_device(t2_stored, v_slab, block_source, r_in):
    slab_count = lax.axis_size("slab")
    rep_count = lax.axis_size("rep")
    slab_index = lax.axis_index("slab")
    rep_index = lax.axis_index("rep")
    row_count = t2_stored.shape[0]
    stored = t2_stored.shape[1] // BLK
    blk_dev = v_slab.shape[1] // BLK
    nblk_total = blk_dev * slab_count
    capacity = max(2, stored // slab_count)
    owner, slot_rank = block_maps(block_source, nblk_total, stored, blk_dev)
    local_ids = slab_index * blk_dev + jnp.arange(blk_dev, dtype=jnp.int32)
    stored_ids = jnp.take(block_source, local_ids)
    source_holder = stored_ids // stored
    source_rank = jnp.take(slot_rank, stored_ids)
    own_blocks = (slab_index * rep_count + rep_index) * stored + jnp.arange(stored, dtype=jnp.int32)
    owners_here = jnp.take(owner, own_blocks)
    ranks_here = jnp.take(slot_rank, own_blocks)
    wanted = (
        owners_here[None, None, :] == jnp.arange(slab_count, dtype=jnp.int32)[:, None, None]
    ) & (ranks_here[None, None, :] == jnp.arange(capacity, dtype=jnp.int32)[None, :, None])
    chosen = jnp.sum(
        jnp.where(wanted, jnp.arange(stored, dtype=jnp.int32)[None, None, :], 0), axis=2
    )
    filled = jnp.any(wanted, axis=2)
    blocked = t2_stored.reshape(row_count, stored, BLK)
    picked = jnp.take(blocked, chosen.reshape(-1), axis=1)
    outgoing = jnp.where(filled.reshape(1, -1, 1), picked, 0.0).reshape(
        row_count, slab_count, capacity, BLK
    )
    arrived = lax.all_to_all(outgoing, "slab", split_axis=1, concat_axis=1, tiled=True)
    copies = lax.all_gather(arrived, "rep", axis=1, tiled=True)
    src_slab = source_holder // rep_count
    src_rep = source_holder % rep_count
    slot_ids = (src_rep * slab_count + src_slab) * capacity + source_rank
    ordered = jnp.take(copies.reshape(row_count, -1, BLK), slot_ids, axis=1).reshape(
        row_count, blk_dev * BLK
    )
    partial_value = lax.dot_general(
        ordered,
        v_slab,
        (((1,), (1,)), ((), ())),
        precision=lax.Precision.HIGHEST,
        preferred_element_type=jnp.float32,
    )
    portion = lax.psum_scatter(partial_value, "slab", scatter_dimension=0, tiled=True)
    return r_in + portion


def solution(mesh):
    in_specs = (P("row", ("slab", "rep")), P("rep", "slab"), P(), P(("row", "slab"), "rep"))
    out_specs = P(("row", "slab"), "rep")
    return jax.shard_map(
        per_device, mesh=mesh, in_specs=in_specs, out_specs=out_specs, check_vma=False
    )
```

profile of v0, /device:TPU:1, one launch (start us, length us, event | category | flops | bytes accessed | tf_op | source)
XLA Modules:
  0.0 297.4 jit_solution(9427770246222348303)
XLA Ops:
  6.5 0.0 all-gather.2.cloned.1.call-start
  6.6 0.8 select_reduce_fusion
  7.4 0.3 convert_reduce_fusion
  7.7 0.7 gather_fusion.4
  8.3 0.7 gather_fusion.5
  9.0 0.1 iota_compare_fusion.2
  9.1 0.1 iota_compare_fusion.3
  9.2 0.1 fusion.1
  9.3 0.1 copy.15
  9.4 0.1 and_reduce_fusion
  9.4 0.1 reshape.162
  9.6 3.2 %copy.14 = f32[512,1280]{0,1:T(8,128)} copy(f32[512,1280]{1,0:T(8,128)} %param.8) | data formatting | bytes 5242880 | tf_op args[0]
  12.8 2.1 copy.16
  14.9 0.1 copy.13
  15.0 0.1 copy.12
  15.1 4.3 %gather_fusion = f32[32,512,128]{2,1,0:T(8,128)} fusion(f32[512,10,128]{2,0,1:T(8,128)S(1)} %copy.16, s32[1024]{0:T(1024)S(1)} %pad_clamp_fusion.1), kind=kCustom, calls=%fused_computation.4 | custom fusion | bytes 16777344 | tf_op jit(solution)/shard_map/jit(_take)/gather | solution.py:50
  19.4 5.2 %select_select_fusion = f32[512,16,2,128]{3,0,2,1:T(8,128)S(1)} fusion(f32[512,16,2,128]{3,0,2,1:T(8,128)} %bitcast.14, pred[16,2]{1,0:T(8,128)(4,1)S(1)} %copy.13, pred[16,2]{1,0:T(8,128)(4,1)S(1)} %copy.12), kind=kLoop, calls=%fused_computation.6 | loop fusion | flops 4194304 | bytes 16777280 | tf_op jit(solution)/shard_map/jit(_where)/select_n | solution.py:51
  24.6 102.2 %all_to_all.5 = f32[512,16,2,128]{3,0,2,1:T(8,128)} all-to-all(f32[512,16,2,128]{3,0,2,1:T(8,128)S(1)} %select_select_fusion), channel_id=1, replica_groups=mesh['row'=8,'slab'=16,'rep'=2] {'slab'}, dimensions={1} | all-to-all | bytes 16777216 | tf_op jit(solution)/shard_map/all_to_all | solution.py:54
  126.8 0.0 copy-start
  126.8 0.0 all-gather.2.cloned.1.call-update
  126.8 0.2 reduce-scatter.2.cloned.1.call-start
  127.1 0.4 copy-done
  127.5 0.7 gather_fusion.2
  128.2 0.7 gather_fusion.3
  129.0 0.1 broadcast_bitcast_fusion
  129.1 36.1 %all-gather.2.cloned.1.call-done = f32[512,32,2,128]{3,0,2,1:T(8,128)} async-done(((f32[512,16,2,128]{3,0,2,1:T(8,128)}), f32[512,32,2,128]{3,0,2,1:T(8,128)}) %all-gather.2.cloned.1.call-update) | async-done | bytes 16777232 | tf_op jit(solution)/shard_map/all_gather | solution.py:55
  165.2 9.0 %gather_fusion.1 = f32[20,512,128]{2,1,0:T(8,128)} fusion(f32[512,64,128]{2,0,1:T(8,128)} %bitcast.17, s32[1024]{0:T(1024)S(1)} %pad_clamp_fusion), kind=kCustom, calls=%fused_computation.5 | custom fusion | bytes 10485840 | tf_op jit(solution)/shard_map/jit(_take)/gather | solution.py:59
  174.2 5.9 %copy.17 = f32[512,20,128]{0,2,1:T(8,128)} copy(f32[512,20,128]{2,0,1:T(8,128)} %bitcast.15) | data formatting | bytes 10485760 | tf_op jit(solution)/shard_map/jit(_take)/gather | solution.py:59
  180.1 3.2 %bitcast_select_fusion = f32[512,2560]{0,1:T(8,128)S(1)} fusion(f32[512,20,128]{0,2,1:T(8,128)} %copy.17, pred[2560]{0:T(1024)(128)(4,1)S(1)} %broadcast_bitcast_fusion), kind=kLoop, calls=%fused_computation.7 | loop fusion | flops 1310720 | bytes 10488320 | tf_op jit(solution)/shard_map/jit(_take)/select_n | solution.py:59
  183.3 0.0 copy-start.1
  183.3 28.0 %fusion.10 = f32[512,768]{1,0:T(8,128)} fusion(f32[512,2560]{0,1:T(8,128)S(1)} %bitcast_select_fusion, f32[768,2560]{1,0:T(8,128)} %param.9), kind=kOutput, calls=%fused_computation.58 | convolution fusion | flops 12079595520 | bytes 14680064 | tf_op jit(solution)/shard_map/dot_general | solution.py:62
  211.3 0.0 reduce-scatter.2.cloned.1.call-update
  211.3 77.7 %reduce-scatter.2.cloned.1.call-done = f32[32,768]{1,0:T(8,128)} async-done(((f32[512,768]{1,0:T(8,128)}), f32[32,768]{1,0:T(8,128)}) %reduce-scatter.2.cloned.1.call-update) | async-done | bytes 98320 | tf_op jit(solution)/shard_map/reduce_scatter | solution.py:69
  289.0 0.0 copy-done.1
  289.0 1.5 add.97
  (14 shorter events, 0.1 us)
Async XLA Ops:
  6.5 158.7 %all-gather.2.cloned.1.call-start = ((), (), s32[]{:S(2)}) async-start(), calls=%async_computation.2 | async-start | bytes 25165824 | tf_op jit(solution)/shard_map/all_gather | solution.py:55
  126.8 0.7 copy-start
  126.8 162.2 %reduce-scatter.2.cloned.1.call-start = ((), (), s32[]{:S(2)}) async-start(), calls=%async_computation.3 | async-start | bytes 1671168 | tf_op jit(solution)/shard_map/reduce_scatter | solution.py:69
  183.3 105.7 %copy-start.1 = (f32[32,768]{1,0:T(8,128)S(1)}, f32[32,768]{1,0:T(8,128)}, u32[]{:S(2)}) copy-start(f32[32,768]{1,0:T(8,128)} %param.11) | copy-start | bytes 294916
Sparse Core Ops, SparseCore 0:
  127.0 38.1 all-gather.1
  211.5 77.5 reduce-scatter.1
where the time goes:
time: 298 us; the launch traced here: 297 us
  waiting for transfers between devices  114 us (38%)
  blocking collectives  102 us (34%)
  local copies, waits for them, and re-layouts  28.2 us (9%)
  matrix products  28 us (9%)
  between operations  13.5 us (5%)
  other arithmetic  11.5 us (4%)
    all_to_all x1, blocking collectives, per_device(): lax.all_to_all(outgoing, 'slab', split_axis=1, concat_axis=1, tiled=True)  102 us
    reduce_scatter x1, waiting for transfers between devices, per_device(): lax.psum_scatter(partial_value, 'slab', scatter_dimension=0, tiled=True)  77.7 us
    all_gather x1, waiting for transfers between devices, per_device(): copies = lax.all_gather(arrived, 'rep', axis=1, tiled=True)  36.1 us
    dot_general x1, matrix products, per_device(): lax.dot_general(ordered, v_slab, (((1,), (1,)), ((), ())), precision=lax....  28 us
    gather x2, local copies, waits for them, and re-layouts, per_device(): jnp.take(copies.reshape(row_count, -1, BLK), slot_ids, axis=1)  14.9 us
  transfers between devices with their start and end apart: 2, of which 2 were waited for; matrix products, arithmetic and copies ran while one was open for 1% of the time, Pallas kernels for 0%

commit v1 on v0

v1 whole, which is shorter than its diff:
```python
import jax
import jax.numpy as jnp
from jax import lax
from jax.experimental import pallas as pl
from jax.experimental.pallas import tpu as pltpu
from jax.sharding import PartitionSpec as P

BLK = 128
SIDE = 4
SLABS = 16
CHUNKS = 2
ROWS = 8
MESH = pl.DeviceIdType.MESH


def hops(da, db):
    return min(da, SIDE - da) + min(db, SIDE - db)


SHIFTS = sorted(
    [(da, db) for da in range(SIDE) for db in range(SIDE)],
    key=lambda d: -hops(*d),
)


def slot(da, db):
    return da * SIDE + db


def kernel(
    source_ref, t2_ref, v_ref, r_ref, out_ref,
    v_raw, v_hi, v_lo, part_a, part_b, send_buf, whole, split, ladder, level1, summed, level2,
    v_sem, own_sem, send1, recv1, send2, recv2, send3, recv3, send4, recv4, send5, recv5,
):
    row = lax.axis_index("row")
    slab = lax.axis_index("slab")
    core = lax.axis_index("rep")
    x, y = slab // SIDE, slab % SIDE
    a = x + core * (y - x)
    b = y + core * (x - y)
    stored = t2_ref.shape[1]
    owned = v_ref.shape[1] // BLK
    strip = CHUNKS * ROWS
    parts = (part_a, part_b)

    def slab_at(da, db):
        aa, bb = (a + da + SIDE) % SIDE, (b + db + SIDE) % SIDE
        xx, yy = aa + core * (bb - aa), bb + core * (aa - bb)
        return xx * SIDE + yy

    def device(da, db, flip=0):
        return (row, slab_at(da, db), (core + flip) % 2)

    v_copy = pltpu.make_async_copy(v_ref, v_raw, v_sem)
    v_copy.start()

    def spread(chunk, da, db, flip):
        to_slab = slab_at(da, db)
        to_core = (core + flip) % 2
        rows = t2_ref.at[(to_slab * 2 + to_core) * CHUNKS + chunk]
        here = pl.ds((slab * 2 + core) * stored, stored)
        n = slot(da, db) * 2 + flip
        if da == 0 and db == 0 and flip == 0:
            return pltpu.make_async_copy(rows, parts[chunk].at[here], own_sem.at[chunk])
        return pltpu.make_async_remote_copy(
            src_ref=rows,
            dst_ref=parts[chunk].at[here],
            send_sem=send1.at[chunk, n],
            recv_sem=recv1.at[chunk, n],
            device_id=device(da, db, flip),
            device_id_type=MESH,
        )

    def spread_arrival(chunk, da, db, flip):
        from_slab = slab_at(-da, -db)
        n = slot(da, db) * 2 + flip
        if flip:
            from_slab = slab_at(-db, -da)
        there = pl.ds((from_slab * 2 + (core + flip) % 2) * stored, stored)
        return pltpu.make_async_remote_copy(
            src_ref=parts[chunk].at[there],
            dst_ref=parts[chunk].at[there],
            send_sem=send1.at[chunk, n],
            recv_sem=recv1.at[chunk, n],
            device_id=device(da, db, flip),
            device_id_type=MESH,
        )

    def collect(chunk, da, db):
        n = slot(da, db)
        return pltpu.make_async_remote_copy(
            src_ref=send_buf.at[chunk, n],
            dst_ref=whole.at[chunk, pl.ds(n * strip, ROWS)],
            send_sem=send2.at[chunk, n],
            recv_sem=recv2.at[chunk, n],
            device_id=device(da, db),
            device_id_type=MESH,
        )

    def share(chunk, da, db):
        return pltpu.make_async_remote_copy(
            src_ref=whole.at[chunk, pl.ds(slot(da, db) * strip, ROWS)],
            dst_ref=whole.at[chunk, pl.ds(slot(db, da) * strip + ROWS, ROWS)],
            send_sem=send3.at[chunk, slot(da, db)],
            recv_sem=recv3.at[chunk, slot(da, db)],
            device_id=device(0, 0, 1),
            device_id_type=MESH,
        )

    def first_sum(chunk, da):
        rows = SIDE * strip
        return pltpu.make_async_remote_copy(
            src_ref=ladder.at[chunk, pl.ds(da * rows, rows)],
            dst_ref=level1.at[chunk, da - 1],
            send_sem=send4.at[chunk, da - 1],
            recv_sem=recv4.at[chunk, da - 1],
            device_id=device(-da, 0),
            device_id_type=MESH,
        )

    def second_sum(chunk, db):
        return pltpu.make_async_remote_copy(
            src_ref=summed.at[chunk, pl.ds(db * strip, strip)],
            dst_ref=level2.at[chunk, db - 1],
            send_sem=send5.at[chunk, db - 1],
            recv_sem=recv5.at[chunk, db - 1],
            device_id=device(0, -db),
            device_id_type=MESH,
        )

    barrier = pltpu.get_barrier_semaphore()
    for da, db in SHIFTS:
        for flip in range(2):
            if (da, db, flip) != (0, 0, 0):
                pl.semaphore_signal(
                    barrier, inc=1, device_id=device(da, db, flip), device_id_type=MESH
                )
    pl.semaphore_wait(barrier, 2 * SLABS - 1)

    for chunk in range(CHUNKS):
        for da, db in SHIFTS:
            for flip in range(2):
                spread(chunk, da, db, flip).start()

    v_copy.wait()
    tile = 64

    @pl.loop(0, v_raw.shape[0] // tile)
    def _(n):
        at = pl.ds(pl.multiple_of(n * tile, tile), tile)
        value = v_raw[at, :]
        high = value.astype(jnp.bfloat16)
        v_hi[at, :] = high
        v_lo[at, :] = (value - high.astype(jnp.float32)).astype(jnp.bfloat16)

    for chunk in range(CHUNKS):
        for da, db in SHIFTS:
            for flip in range(2):
                if (da, db, flip) == (0, 0, 0):
                    spread(chunk, 0, 0, 0).wait()
                else:
                    spread_arrival(chunk, da, db, flip).wait_recv()
        for da, db in SHIFTS:
            first = slab_at(da, db) * owned
            for k in range(owned):
                piece = parts[chunk][source_ref[first + k]]
                if (da, db) == (0, 0):
                    whole[chunk, 0:ROWS, k * BLK:(k + 1) * BLK] = piece
                else:
                    send_buf[chunk, slot(da, db), :, k * BLK:(k + 1) * BLK] = piece
            if (da, db) != (0, 0):
                collect(chunk, da, db).start()
            else:
                share(chunk, 0, 0).start()

    def exchange(chunk):
        for da, db in SHIFTS:
            if (da, db) != (0, 0):
                collect(chunk, da, db).wait_recv()
                share(chunk, da, db).start()

    def multiply(chunk):
        for da, db in SHIFTS:
            share(chunk, da, db).wait_recv()
        m = whole.shape[1]

        @pl.loop(0, m // 32)
        def _(n):
            at = pl.ds(pl.multiple_of(n * 32, 32), 32)
            value = whole[chunk, at, :]
            high = value.astype(jnp.bfloat16)
            split[at, :] = high
            split[pl.ds(pl.multiple_of(m + n * 32, 32), 32), :] = (
                value - high.astype(jnp.float32)
            ).astype(jnp.bfloat16)

        width = 256

        @pl.loop(0, v_hi.shape[0] // width)
        def _(n):
            at = pl.ds(pl.multiple_of(n * width, width), width)
            dims = (((1,), (1,)), ((), ()))
            both = lax.dot_general(
                split[...], v_hi[at, :], dims, preferred_element_type=jnp.float32
            )
            low = lax.dot_general(
                split[0:m, :], v_lo[at, :], dims, preferred_element_type=jnp.float32
            )
            ladder[chunk, :, at] = both[0:m] + (both[m:] + low)

        for da in range(1, SIDE):
            first_sum(chunk, da).start()

    def add_first(chunk):
        rows = SIDE * strip
        for da in range(1, SIDE):
            first_sum(chunk, da).wait_recv()
        summed[chunk] = (ladder[chunk, 0:rows, :] + level1[chunk, 0]) + (
            level1[chunk, 1] + level1[chunk, 2]
        )
        for db in range(1, SIDE):
            second_sum(chunk, db).start()

    def add_second(chunk):
        for db in range(1, SIDE):
            second_sum(chunk, db).wait_recv()
        total = (summed[chunk, 0:strip, :] + level2[chunk, 0]) + (
            level2[chunk, 1] + level2[chunk, 2]
        )
        for part in range(2):
            at = pl.ds(
                pl.multiple_of(((core + part) % 2) * strip + chunk * ROWS, ROWS), ROWS
            )
            out_ref[at, :] = r_ref[at, :] + total[part * ROWS:(part + 1) * ROWS]

    exchange(0)
    multiply(0)
    exchange(1)
    add_first(0)
    multiply(1)
    add_second(0)
    add_first(1)
    add_second(1)

    for chunk in range(CHUNKS):
        for da, db in SHIFTS:
            for flip in range(2):
                if (da, db, flip) != (0, 0, 0):
                    spread(chunk, da, db, flip).wait_send()
            if (da, db) != (0, 0):
                collect(chunk, da, db).wait_send()
            share(chunk, da, db).wait_send()
        for d in range(1, SIDE):
            first_sum(chunk, d).wait_send()
            second_sum(chunk, d).wait_send()


def per_device(t2_stored, v_slab, block_source, r_in):
    blocks = block_source.shape[0]
    tiles = t2_stored.reshape(t2_stored.shape[0] // ROWS, ROWS, -1, BLK).transpose(0, 2, 1, 3)
    ab, cd = v_slab.shape
    strip = CHUNKS * ROWS
    rows = SLABS * strip
    f32, bf16 = jnp.float32, jnp.bfloat16
    dma = pltpu.SemaphoreType.DMA
    return pl.pallas_call(
        kernel,
        out_shape=jax.ShapeDtypeStruct(r_in.shape, f32),
        in_specs=[
            pl.BlockSpec(memory_space=pltpu.SMEM),
            pl.BlockSpec(memory_space=pl.ANY),
            pl.BlockSpec(memory_space=pl.ANY),
            pl.BlockSpec(memory_space=pltpu.VMEM),
        ],
        out_specs=pl.BlockSpec(memory_space=pltpu.VMEM),
        scratch_shapes=[
            pltpu.VMEM((ab, cd), f32),
            pltpu.VMEM((ab, cd), bf16),
            pltpu.VMEM((ab, cd), bf16),
            pltpu.VMEM((blocks, ROWS, BLK), f32),
            pltpu.VMEM((blocks, ROWS, BLK), f32),
            pltpu.VMEM((CHUNKS, SLABS, ROWS, cd), f32),
            pltpu.VMEM((CHUNKS, rows, cd), f32),
            pltpu.VMEM((2 * rows, cd), bf16),
            pltpu.VMEM((CHUNKS, rows, ab), f32),
            pltpu.VMEM((CHUNKS, SIDE - 1, SIDE * strip, ab), f32),
            pltpu.VMEM((CHUNKS, SIDE * strip, ab), f32),
            pltpu.VMEM((CHUNKS, SIDE - 1, strip, ab), f32),
            dma,
            dma((CHUNKS,)),
            dma((CHUNKS, 2 * SLABS)),
            dma((CHUNKS, 2 * SLABS)),
            dma((CHUNKS, SLABS)),
            dma((CHUNKS, SLABS)),
            dma((CHUNKS, SLABS)),
            dma((CHUNKS, SLABS)),
            dma((CHUNKS, SIDE - 1)),
            dma((CHUNKS, SIDE - 1)),
            dma((CHUNKS, SIDE - 1)),
            dma((CHUNKS, SIDE - 1)),
        ],
        compiler_params=pltpu.CompilerParams(
            collective_id=1, has_side_effects=True, vmem_limit_bytes=60 * 1024 * 1024
        ),
        name="ladder",
    )(block_source, tiles, v_slab, r_in)


def solution(mesh):
    in_specs = (P("row", ("slab", "rep")), P("rep", "slab"), P(), P(("row", "slab"), "rep"))
    out_specs = P(("row", "slab"), "rep")
    return jax.shard_map(
        per_device, mesh=mesh, in_specs=in_specs, out_specs=out_specs, check_vma=False
    )
```

time: 298 us -> 97.2 us (0.33)
  waiting for transfers between devices: 114 us -> 0 us
  blocking collectives: 102 us -> 0 us
  Pallas kernels: 0 us -> 93.8 us
  matrix products: 28 us -> 0 us
  local copies, waits for them, and re-layouts: 28.2 us -> 1.54 us
  between operations: 13.5 us -> 0.01 us
  other arithmetic: 11.5 us -> 0 us
    all_to_all x1 -> x0, blocking collectives: 102 us -> none  [per_device(): lax.all_to_all(outgoing, 'slab', split_axis=1, concat_axis=1, tiled=True)]
    pallas_call x0 -> x1, Pallas kernels: none -> 93.8 us  [per_device(): pl.pallas_call(kernel, out_shape=jax.ShapeDtypeStruct(r_in.shape, f32), i...]
    reduce_scatter x1 -> x0, waiting for transfers between devices: 77.7 us -> none  [per_device(): lax.psum_scatter(partial_value, 'slab', scatter_dimension=0, tiled=True)]
    all_gather x1 -> x0, waiting for transfers between devices: 36.1 us -> none  [per_device(): copies = lax.all_gather(arrived, 'rep', axis=1, tiled=True)]
    dot_general x1 -> x0, matrix products: 28 us -> none  [per_device(): lax.dot_general(ordered, v_slab, (((1,), (1,)), ((), ())), precision=lax....]
    gather x7 -> x0, local copies, waits for them, and re-layouts: 22 us -> none  [the longest x2 14.9 us: per_device(): jnp.take(copies.reshape(row_count, -1, BLK), slot_ids, axis=1)]
    select_n x9 -> x0, other arithmetic: 8.43 us -> none  [the longest x1 5.17 us: per_device(): jnp.where(filled.reshape(1, -1, 1), picked, 0.0)]
  transfers between devices with their start and end apart: 2 -> 0, of which waited for: 2 -> 0; matrix products, arithmetic and copies ran while one was open for 1% -> 0% of each run, Pallas kernels for 0% -> 0%
where the time goes in v1:
time: 97.2 us; the launch traced here: 95.3 us
  Pallas kernels  93.8 us (97%)
  local copies, waits for them, and re-layouts  1.54 us (2%)
    pallas_call x1, Pallas kernels, per_device(): pl.pallas_call(kernel, out_shape=jax.ShapeDtypeStruct(r_in.shape, f32), i...  93.8 us

profile of v1, /device:TPU:1, one launch (start us, length us, event | category | flops | bytes accessed | tf_op | source)
XLA Modules:
  0.0 95.3 jit_solution(6827424719957536910)
XLA Ops:
  0.0 93.8 %ladder.1 = f32[32,768]{1,0:T(8,128)} custom-call(s32[320]{0:T(512)} %source_ref.1, f32[64,10,8,128]{3,2,1,0:T(8,128)} %bitcast.3, f32[768,2560]{1,0:T(8,128)} %v_ref.1, f32[32,768]{1,0:T(8,128)} %r_ref.1), custom_call_target="tpu_custom_call" | custom-call | tf_op jit(solution)/shard_map/ladder/pallas_call | solution.py:266
  93.8 1.5 %copy.6 = f32[32,768]{1,0:T(8,128)} copy(f32[32,768]{1,0:T(8,128)} %ladder.1) | data formatting | bytes 196608

commit v2 on v0

v2 whole, which is shorter than its diff:
```python
import jax
import jax.numpy as jnp
from jax import lax
from jax.experimental import pallas as pl
from jax.experimental.pallas import tpu as pltpu
from jax.sharding import PartitionSpec as P

BLK = 128
SIDE = 4
SLABS = 16
CHUNKS = 2
ROWS = 8
MESH = pl.DeviceIdType.MESH


SHIFTS = (2, 1, 3)
WIDTH = 256


def kernel(
    place_ref, t2_ref, v_ref, out_ref,
    v_raw, v_hi, v_lo, relay1, part_a, part_b, send_buf, relay2, whole, split,
    ladder, level1, summed, level2,
    v_sem, own_sem, send1, recv1, send2, recv2, send3, recv3, send4, recv4,
    send5, recv5, send6, recv6, send7, recv7,
):
    row = lax.axis_index("row")
    slab = lax.axis_index("slab")
    core = lax.axis_index("rep")
    x, y = slab // SIDE, slab % SIDE
    a = x + core * (y - x)
    b = y + core * (x - y)
    stored = t2_ref.shape[3]
    owned = v_ref.shape[1] // BLK
    ab = v_ref.shape[0]
    strip = 2 * ROWS
    group = SIDE * strip
    parts = (part_a, part_b)

    def slab_at(aa, bb):
        xx, yy = aa + core * (bb - aa), bb + core * (aa - bb)
        return xx * SIDE + yy

    def device(da, db, flip=0):
        return (row, slab_at((a + da + SIDE) % SIDE, (b + db + SIDE) % SIDE), (core + flip) % 2)

    def remote(src, dst, send_sem, recv_sem, da, db, flip=0):
        return pltpu.make_async_remote_copy(
            src_ref=src,
            dst_ref=dst,
            send_sem=send_sem,
            recv_sem=recv_sem,
            device_id=device(da, db, flip),
            device_id_type=MESH,
        )

    def spread_a(chunk, da, to_b):
        src = t2_ref.at[slab_at((a + da) % SIDE, to_b), chunk]
        dst = relay1.at[chunk, to_b, :, pl.ds(a * stored, stored)]
        if da == 0:
            return pltpu.make_async_copy(src, dst, own_sem.at[chunk, to_b])
        return remote(
            src, dst, send1.at[chunk, da - 1, to_b], recv1.at[chunk, da - 1, to_b], da, 0
        )

    def spread_a_arrival(chunk, da, to_b):
        here = relay1.at[chunk, to_b, :, pl.ds(((a - da + SIDE) % SIDE) * stored, stored)]
        return remote(
            here, here, send1.at[chunk, da - 1, to_b], recv1.at[chunk, da - 1, to_b], da, 0
        )

    def spread_b(chunk, db, flip):
        src = relay1.at[chunk, (b + db) % SIDE, (core + flip) % 2]
        n = SIDE * stored
        dst = parts[chunk].at[pl.ds((core * SIDE + b) * n, n)]
        if (db, flip) == (0, 0):
            return pltpu.make_async_copy(src, dst, own_sem.at[chunk, SIDE])
        return remote(
            src, dst, send2.at[chunk, db, flip], recv2.at[chunk, db, flip], 0, db, flip
        )

    def spread_b_arrival(chunk, db, flip):
        n = SIDE * stored
        from_b = ((a if flip else b) - db + SIDE) % SIDE
        here = parts[chunk].at[pl.ds(((core + flip) % 2 * SIDE + from_b) * n, n)]
        return remote(
            here, here, send2.at[chunk, db, flip], recv2.at[chunk, db, flip], 0, db, flip
        )

    def collect_a(chunk, da):
        return remote(
            send_buf.at[chunk, da - 1],
            relay2.at[chunk, :, da],
            send3.at[chunk, da - 1],
            recv3.at[chunk, da - 1],
            da,
            0,
        )

    def collect_b(chunk, db):
        src = relay2.at[chunk, (b + db) % SIDE]
        dst = whole.at[chunk, :, db, 0]
        if db == 0:
            return pltpu.make_async_copy(src, dst, own_sem.at[chunk, SIDE + 1])
        return remote(src, dst, send4.at[chunk, db - 1], recv4.at[chunk, db - 1], 0, db)

    def share(chunk, db):
        src = relay2.at[chunk, b] if db == 0 else whole.at[chunk, :, db, 0]
        return remote(
            src, whole.at[chunk, db, :, 1], send5.at[chunk, db], recv5.at[chunk, db], 0, 0, 1
        )

    def first_sum(chunk, da, n):
        cols = pl.ds(n * WIDTH, WIDTH)
        return remote(
            ladder.at[chunk, da, :, cols],
            level1.at[chunk, da - 1, :, cols],
            send6.at[chunk, da - 1, n],
            recv6.at[chunk, da - 1, n],
            -da,
            0,
        )

    def second_sum(chunk, db):
        return remote(
            summed.at[chunk, pl.ds(db * strip, strip)],
            level2.at[chunk, db - 1],
            send7.at[chunk, db - 1],
            recv7.at[chunk, db - 1],
            0,
            -db,
        )

    def start_spread_a(chunk):
        for da in SHIFTS + (0,):
            for to_b in range(SIDE):
                spread_a(chunk, da, to_b).start()

    def start_spread_b(chunk):
        for to_b in range(SIDE):
            spread_a(chunk, 0, to_b).wait()
            for da in SHIFTS:
                spread_a_arrival(chunk, da, to_b).wait_recv()
        for db in SHIFTS + (0,):
            for flip in range(2):
                spread_b(chunk, db, flip).start()

    def start_collect_a(chunk):
        for db in SHIFTS + (0,):
            for flip in range(2):
                if (db, flip) == (0, 0):
                    spread_b(chunk, 0, 0).wait()
                else:
                    spread_b_arrival(chunk, db, flip).wait_recv()
        for da in SHIFTS + (0,):
            for to_b in range(SIDE):
                first = slab_at((a + da) % SIDE, to_b) * owned
                for k in range(owned):
                    piece = parts[chunk][place_ref[first + k]]
                    cols = slice(k * BLK, (k + 1) * BLK)
                    if da == 0:
                        relay2[chunk, to_b, 0, :, cols] = piece
                    else:
                        send_buf[chunk, da - 1, to_b, :, cols] = piece
            if da:
                collect_a(chunk, da).start()

    def start_collect_b(chunk):
        for da in SHIFTS:
            collect_a(chunk, da).wait_recv()
        for db in SHIFTS + (0,):
            collect_b(chunk, db).start()
        share(chunk, 0).start()

    def start_share(chunk):
        for db in SHIFTS:
            collect_b(chunk, db).wait_recv()
            share(chunk, db).start()
        collect_b(chunk, 0).wait()

    def multiply(chunk):
        for db in (0,) + SHIFTS:
            share(chunk, db).wait_recv()
        m = SIDE * group

        @pl.loop(0, SIDE)
        def _(n):
            value = whole[chunk, n].reshape(group, v_hi.shape[0])
            high = value.astype(jnp.bfloat16)
            at = pl.multiple_of(n * group, group)
            split[pl.ds(at, group), :] = high
            split[pl.ds(pl.multiple_of(m + at, group), group), :] = (
                value - high.astype(jnp.float32)
            ).astype(jnp.bfloat16)

        for n in range(ab // WIDTH):
            cols = slice(n * WIDTH, (n + 1) * WIDTH)
            dims = (((1,), (0,)), ((), ()))
            both = lax.dot_general(
                split[...], v_hi[:, cols], dims, preferred_element_type=jnp.float32
            )
            low = lax.dot_general(
                split[0:m, :], v_lo[:, cols], dims, preferred_element_type=jnp.float32
            )
            ladder[chunk, :, :, cols] = (both[0:m] + (both[m:] + low)).reshape(
                SIDE, group, WIDTH
            )
            for da in SHIFTS:
                first_sum(chunk, da, n).start()

    def add_first(chunk):
        for n in range(ab // WIDTH):
            for da in SHIFTS:
                first_sum(chunk, da, n).wait_recv()
            cols = slice(n * WIDTH, (n + 1) * WIDTH)
            summed[chunk, :, cols] = (ladder[chunk, 0, :, cols] + level1[chunk, 0, :, cols]) + (
                level1[chunk, 1, :, cols] + level1[chunk, 2, :, cols]
            )
        for db in SHIFTS:
            second_sum(chunk, db).start()

    def add_second(chunk):
        for db in SHIFTS:
            second_sum(chunk, db).wait_recv()
        total = (summed[chunk, 0:strip, :] + level2[chunk, 0]) + (
            level2[chunk, 1] + level2[chunk, 2]
        )
        for part in range(2):
            at = pl.ds(
                pl.multiple_of(chunk * strip + ((core + part) % 2) * ROWS, ROWS), ROWS
            )
            out_ref[at, :] = total[part * ROWS:(part + 1) * ROWS]

    v_copy = pltpu.make_async_copy(v_ref, v_raw, v_sem)
    v_copy.start()

    barrier = pltpu.get_barrier_semaphore()
    greeted = [(d, 0, 0) for d in SHIFTS] + [(0, d, f) for d in SHIFTS for f in range(2)]
    greeted += [(0, 0, 1)] + [(d, 0, 1) for d in SHIFTS]
    for da, db, flip in greeted:
        pl.semaphore_signal(barrier, inc=1, device_id=device(da, db, flip), device_id_type=MESH)
    pl.semaphore_wait(barrier, len(greeted))

    start_spread_a(0)

    v_copy.wait()
    tile = 256

    @pl.loop(0, v_raw.shape[1] // tile)
    def _(n):
        cd = pl.ds(pl.multiple_of(n * tile, tile), tile)
        for m in range(0, v_raw.shape[0], tile):
            value = v_raw[m:m + tile, cd]
            high = value.astype(jnp.bfloat16)
            low = (value - high.astype(jnp.float32)).astype(jnp.bfloat16)
            v_hi[cd, m:m + tile] = high.T
            v_lo[cd, m:m + tile] = low.T

    start_spread_a(1)
    for step in (start_spread_b, start_collect_a, start_collect_b):
        for chunk in range(CHUNKS):
            step(chunk)
    start_share(0)
    multiply(0)
    start_share(1)
    add_first(0)
    multiply(1)
    add_second(0)
    add_first(1)
    add_second(1)

    for chunk in range(CHUNKS):
        for d in SHIFTS:
            for to_b in range(SIDE):
                spread_a(chunk, d, to_b).wait_send()
            for flip in range(2):
                spread_b(chunk, d, flip).wait_send()
            collect_a(chunk, d).wait_send()
            collect_b(chunk, d).wait_send()
            share(chunk, d).wait_send()
            for n in range(ab // WIDTH):
                first_sum(chunk, d, n).wait_send()
            second_sum(chunk, d).wait_send()
        spread_b(chunk, 0, 1).wait_send()
        share(chunk, 0).wait_send()


def per_device(t2_stored, v_slab, block_source, r_in):
    ab, cd = v_slab.shape
    blocks = block_source.shape[0]
    stored = t2_stored.shape[1] // BLK
    owned = cd // BLK
    tiles = t2_stored.reshape(-1, ROWS, stored, BLK).transpose(0, 2, 1, 3)
    tiles = tiles.reshape(SLABS, CHUNKS, 2, stored, ROWS, BLK)
    holder = block_source // stored
    core = holder % 2
    x, y = holder // (2 * SIDE), holder // 2 % SIDE
    a, b = jnp.where(core == 0, x, y), jnp.where(core == 0, y, x)
    place = ((core * SIDE + b) * SIDE + a) * stored + block_source % stored
    strip = 2 * ROWS
    group = SIDE * strip
    f32, bf16 = jnp.float32, jnp.bfloat16
    dma = pltpu.SemaphoreType.DMA
    widths = ab // WIDTH
    ladder = pl.pallas_call(
        kernel,
        out_shape=jax.ShapeDtypeStruct(r_in.shape, f32),
        in_specs=[
            pl.BlockSpec(memory_space=pltpu.SMEM),
            pl.BlockSpec(memory_space=pl.ANY),
            pl.BlockSpec(memory_space=pl.ANY),
        ],
        out_specs=pl.BlockSpec(memory_space=pltpu.VMEM),
        scratch_shapes=[
            pltpu.VMEM((ab, cd), f32),
            pltpu.VMEM((cd, ab), bf16),
            pltpu.VMEM((cd, ab), bf16),
            pltpu.VMEM((CHUNKS, SIDE, 2, SIDE * stored, ROWS, BLK), f32),
            pltpu.VMEM((blocks, ROWS, BLK), f32),
            pltpu.VMEM((blocks, ROWS, BLK), f32),
            pltpu.VMEM((CHUNKS, SIDE - 1, SIDE, ROWS, cd), f32),
            pltpu.VMEM((CHUNKS, SIDE, SIDE, ROWS, cd), f32),
            pltpu.VMEM((CHUNKS, SIDE, SIDE, 2, ROWS, cd), f32),
            pltpu.VMEM((2 * SIDE * group, cd), bf16),
            pltpu.VMEM((CHUNKS, SIDE, group, ab), f32),
            pltpu.VMEM((CHUNKS, SIDE - 1, group, ab), f32),
            pltpu.VMEM((CHUNKS, group, ab), f32),
            pltpu.VMEM((CHUNKS, SIDE - 1, strip, ab), f32),
            dma,
            dma((CHUNKS, SIDE + 2)),
            dma((CHUNKS, SIDE - 1, SIDE)),
            dma((CHUNKS, SIDE - 1, SIDE)),
            dma((CHUNKS, SIDE, 2)),
            dma((CHUNKS, SIDE, 2)),
            dma((CHUNKS, SIDE - 1)),
            dma((CHUNKS, SIDE - 1)),
            dma((CHUNKS, SIDE - 1)),
            dma((CHUNKS, SIDE - 1)),
            dma((CHUNKS, SIDE)),
            dma((CHUNKS, SIDE)),
            dma((CHUNKS, SIDE - 1, widths)),
            dma((CHUNKS, SIDE - 1, widths)),
            dma((CHUNKS, SIDE - 1)),
            dma((CHUNKS, SIDE - 1)),
        ],
        compiler_params=pltpu.CompilerParams(
            collective_id=1, has_side_effects=True, vmem_limit_bytes=60 * 1024 * 1024
        ),
        name="ladder",
    )(place, tiles, v_slab)
    return r_in + ladder


def solution(mesh):
    in_specs = (P("row", ("slab", "rep")), P("rep", "slab"), P(), P(("row", "slab"), "rep"))
    out_specs = P(("row", "slab"), "rep")
    return jax.shard_map(
        per_device, mesh=mesh, in_specs=in_specs, out_specs=out_specs, check_vma=False
    )
```

time: 298 us -> 96.4 us (0.32)
  waiting for transfers between devices: 114 us -> 0 us
  blocking collectives: 102 us -> 0 us
  Pallas kernels: 0 us -> 92.7 us
  local copies, waits for them, and re-layouts: 28.2 us -> 0.01 us
  matrix products: 28 us -> 0 us
  between operations: 13.5 us -> 0.02 us
  other arithmetic: 11.5 us -> 2.87 us
    all_to_all x1 -> x0, blocking collectives: 102 us -> none  [per_device(): lax.all_to_all(outgoing, 'slab', split_axis=1, concat_axis=1, tiled=True)]
    pallas_call x0 -> x1, Pallas kernels: none -> 92.7 us  [per_device(): pl.pallas_call(kernel, out_shape=jax.ShapeDtypeStruct(r_in.shape, f32), i...]
    reduce_scatter x1 -> x0, waiting for transfers between devices: 77.7 us -> none  [per_device(): lax.psum_scatter(partial_value, 'slab', scatter_dimension=0, tiled=True)]
    all_gather x1 -> x0, waiting for transfers between devices: 36.1 us -> none  [per_device(): copies = lax.all_gather(arrived, 'rep', axis=1, tiled=True)]
    dot_general x1 -> x0, matrix products: 28 us -> none  [per_device(): lax.dot_general(ordered, v_slab, (((1,), (1,)), ((), ())), precision=lax....]
    gather x7 -> x0, local copies, waits for them, and re-layouts: 22 us -> none  [the longest x2 14.9 us: per_device(): jnp.take(copies.reshape(row_count, -1, BLK), slot_ids, axis=1)]
    select_n x9 -> x0, other arithmetic: 8.43 us -> none  [the longest x1 5.17 us: per_device(): jnp.where(filled.reshape(1, -1, 1), picked, 0.0)]
    unnamed x5 -> x2, local copies, waits for them, and re-layouts: 3.63 us -> 0.01 us
  transfers between devices with their start and end apart: 2 -> 0, of which waited for: 2 -> 0; matrix products, arithmetic and copies ran while one was open for 1% -> 0% of each run, Pallas kernels for 0% -> 0%
where the time goes in v2:
time: 96.4 us; the launch traced here: 95.6 us
  Pallas kernels  92.7 us (96%)
  other arithmetic  2.87 us (3%)
    pallas_call x1, Pallas kernels, per_device(): pl.pallas_call(kernel, out_shape=jax.ShapeDtypeStruct(r_in.shape, f32), i...  92.7 us

profile of v2, /device:TPU:1, one launch (start us, length us, event | category | flops | bytes accessed | tf_op | source)
XLA Modules:
  0.0 95.6 jit_solution(4213052455044833856)
XLA Ops:
  0.0 0.0 copy-start
  0.0 1.3 %fusion.2.place_ref = s32[320]{0:T(512)} fusion(s32[320]{0:T(512)} %param.6), kind=kLoop, calls=%fused_computation.15 | loop fusion | flops 19520 | bytes 2560 | tf_op jit(solution)/shard_map/add | solution.py:299
  1.3 92.7 %ladder.1 = f32[32,768]{1,0:T(8,128)} custom-call(s32[320]{0:T(512)} %fusion.2.place_ref, f32[16,2,2,10,8,128]{5,4,3,2,1,0:T(8,128)} %bitcast.5, f32[768,2560]{1,0:T(8,128)} %v_ref.1), custom_call_target="tpu_custom_call" | custom-call | tf_op jit(solution)/shard_map/ladder/pallas_call | solution.py:305
  94.0 0.0 copy-done
  94.0 1.5 %add.35 = f32[32,768]{1,0:T(8,128)} add(f32[32,768]{1,0:T(8,128)S(1)} %copy-done, f32[32,768]{1,0:T(8,128)} %ladder.1) | non-fusion elementwise | flops 24576 | bytes 294912 | tf_op jit(solution)/shard_map/add | solution.py:351
Async XLA Ops:
  0.0 94.0 %copy-start = (f32[32,768]{1,0:T(8,128)S(1)}, f32[32,768]{1,0:T(8,128)}, u32[]{:S(2)}) copy-start(f32[32,768]{1,0:T(8,128)} %param.7) | copy-start | bytes 294916

commit v3 on v0

v3 whole, which is shorter than its diff:
```python
import jax
import jax.numpy as jnp
from jax import lax
from jax.experimental import pallas as pl
from jax.experimental.pallas import tpu as pltpu
from jax.sharding import PartitionSpec as P

BLK = 128
SIDE = 4
SLABS = 16
CHUNKS = 2
ROWS = 8
MESH = pl.DeviceIdType.MESH


SHIFTS = (2, 1, 3)
ARRIVALS = (2, 1, 3)
SPREAD = sorted(
    [(da, db) for da in range(SIDE) for db in range(SIDE)],
    key=lambda d: -sum(min(n, SIDE - n) for n in d),
)
GROUPS = (2, 1, 3, 0)


def kernel(
    source_ref, t2_ref, v_ref, out_ref,
    v_raw, v_hi, v_lo, part_a, part_b, send_buf, relay2, whole, split,
    ladder, level1, summed, level2,
    v_sem, own_sem, send1, recv1, send3, recv3, send4, recv4,
    send5, recv5, send6, recv6, send7, recv7,
):
    row = lax.axis_index("row")
    slab = lax.axis_index("slab")
    core = lax.axis_index("rep")
    x, y = slab // SIDE, slab % SIDE
    a = x + core * (y - x)
    b = y + core * (x - y)
    stored = t2_ref.shape[3]
    owned = v_ref.shape[1] // BLK
    group = SIDE * ROWS
    parts = (part_a, part_b)

    def slab_at(aa, bb):
        xx, yy = aa + core * (bb - aa), bb + core * (aa - bb)
        return xx * SIDE + yy

    def device(da, db, flip=0):
        return (row, slab_at((a + da + SIDE) % SIDE, (b + db + SIDE) % SIDE), (core + flip) % 2)

    def remote(src, dst, send_sem, recv_sem, da, db, flip=0):
        return pltpu.make_async_remote_copy(
            src_ref=src,
            dst_ref=dst,
            send_sem=send_sem,
            recv_sem=recv_sem,
            device_id=device(da, db, flip),
            device_id_type=MESH,
        )

    def spread(chunk, da, db, flip):
        to_slab = slab_at((a + da) % SIDE, (b + db) % SIDE)
        src = t2_ref.at[to_slab, chunk, (core + flip) % 2]
        dst = parts[chunk].at[pl.ds((slab * 2 + core) * stored, stored)]
        if (da, db, flip) == (0, 0, 0):
            return pltpu.make_async_copy(src, dst, own_sem.at[chunk, 0])
        n = (da * SIDE + db) * 2 + flip
        return remote(src, dst, send1.at[chunk, n], recv1.at[chunk, n], da, db, flip)

    def spread_arrival(chunk, da, db, flip):
        ea, eb = (db, da) if flip else (da, db)
        from_slab = slab_at((a - ea + SIDE) % SIDE, (b - eb + SIDE) % SIDE)
        here = parts[chunk].at[pl.ds((from_slab * 2 + (core + flip) % 2) * stored, stored)]
        n = (da * SIDE + db) * 2 + flip
        return remote(here, here, send1.at[chunk, n], recv1.at[chunk, n], da, db, flip)

    def collect_a(chunk, da):
        return remote(
            send_buf.at[chunk, da - 1],
            relay2.at[chunk, :, da],
            send3.at[chunk, da - 1],
            recv3.at[chunk, da - 1],
            da,
            0,
        )

    def collect_b(chunk, da, db):
        src = relay2.at[chunk, (b + db) % SIDE, da]
        dst = whole.at[chunk, 0, da, db]
        if db == 0:
            return pltpu.make_async_copy(src, dst, own_sem.at[chunk, SIDE + da])
        n = db - 1
        return remote(src, dst, send4.at[chunk, da, n], recv4.at[chunk, da, n], 0, db)

    def share(chunk, da, db):
        src = relay2.at[chunk, b, da] if db == 0 else whole.at[chunk, 0, da, db]
        dst = whole.at[chunk, 1, da, db]
        return remote(src, dst, send5.at[chunk, da, db], recv5.at[chunk, da, db], 0, 0, 1)

    def first_sum(chunk, part, d):
        return remote(
            ladder.at[chunk, part, d],
            level1.at[chunk, part, d - 1],
            send6.at[chunk, part, d - 1],
            recv6.at[chunk, part, d - 1],
            *((-d, 0), (0, -d))[part],
        )

    def second_sum(chunk, part, d):
        return remote(
            summed.at[chunk, part, pl.ds(d * ROWS, ROWS)],
            level2.at[chunk, part, d - 1],
            send7.at[chunk, part, d - 1],
            recv7.at[chunk, part, d - 1],
            *((0, -d), (-d, 0))[part],
        )

    def start_spread(chunk):
        for da, db in SPREAD:
            for flip in range(2):
                spread(chunk, da, db, flip).start()

    def forward_blocks(chunk, da):
        for db in SHIFTS + (0,):
            collect_b(chunk, da, db).start()
        share(chunk, da, 0).start()

    def start_collect(chunk):
        for da, db in SPREAD:
            for flip in range(2):
                if (da, db, flip) == (0, 0, 0):
                    spread(chunk, 0, 0, 0).wait()
                else:
                    spread_arrival(chunk, da, db, flip).wait_recv()
        for da in SHIFTS + (0,):
            for to_b in range(SIDE):
                first = slab_at((a + da) % SIDE, to_b) * owned
                for k in range(owned):
                    piece = parts[chunk][source_ref[first + k]]
                    cols = slice(k * BLK, (k + 1) * BLK)
                    if da == 0:
                        relay2[chunk, to_b, 0, :, cols] = piece
                    else:
                        send_buf[chunk, da - 1, to_b, :, cols] = piece
            if da:
                collect_a(chunk, da).start()
        forward_blocks(chunk, 0)

    def forward_collect(chunk):
        for da in ARRIVALS:
            collect_a(chunk, da).wait_recv()
            forward_blocks(chunk, da)

    def exchange(chunk, da):
        for db in ARRIVALS:
            collect_b(chunk, da, db).wait_recv()
            share(chunk, da, db).start()

    def multiply(chunk, da):
        collect_b(chunk, da, 0).wait()
        for db in range(SIDE):
            share(chunk, da, db).wait_recv()
        value = whole[chunk, :, da].reshape(2 * group, v_hi.shape[0])
        high = value.astype(jnp.bfloat16)
        split[0:2 * group, :] = high
        split[2 * group:, :] = (value - high.astype(jnp.float32)).astype(jnp.bfloat16)
        dims = (((1,), (0,)), ((), ()))
        both = lax.dot_general(
            split[...], v_hi[...], dims, preferred_element_type=jnp.float32
        )
        low = lax.dot_general(
            split[0:2 * group, :], v_lo[...], dims, preferred_element_type=jnp.float32
        )
        total = both[0:2 * group] + (both[2 * group:] + low)
        for part in range(2):
            ladder[chunk, part, da] = total[part * group:(part + 1) * group]
            if da:
                first_sum(chunk, part, da).start()

    def add_first(chunk):
        for part in range(2):
            for d in ARRIVALS:
                first_sum(chunk, part, d).wait_recv()
            summed[chunk, part] = (ladder[chunk, part, 0] + level1[chunk, part, 0]) + (
                level1[chunk, part, 1] + level1[chunk, part, 2]
            )
            for d in SHIFTS:
                second_sum(chunk, part, d).start()

    def add_second(chunk):
        for part in range(2):
            for d in SHIFTS:
                second_sum(chunk, part, d).wait_recv()
            at = pl.ds(
                pl.multiple_of((chunk * 2 + (core + part) % 2) * ROWS, ROWS), ROWS
            )
            out_ref[at, :] = (summed[chunk, part, 0:ROWS, :] + level2[chunk, part, 0]) + (
                level2[chunk, part, 1] + level2[chunk, part, 2]
            )

    v_copy = pltpu.make_async_copy(v_ref, v_raw, v_sem)
    v_copy.start()

    barrier = pltpu.get_barrier_semaphore()
    for da, db in SPREAD:
        for flip in range(2):
            if (da, db, flip) != (0, 0, 0):
                pl.semaphore_signal(
                    barrier, inc=1, device_id=device(da, db, flip), device_id_type=MESH
                )
    pl.semaphore_wait(barrier, 2 * SLABS - 1)

    start_spread(0)
    start_spread(1)

    v_copy.wait()
    tile = 256

    @pl.loop(0, v_raw.shape[1] // tile)
    def _(n):
        cd = pl.ds(pl.multiple_of(n * tile, tile), tile)
        for m in range(0, v_raw.shape[0], tile):
            value = v_raw[m:m + tile, cd]
            high = value.astype(jnp.bfloat16)
            low = (value - high.astype(jnp.float32)).astype(jnp.bfloat16)
            v_hi[cd, m:m + tile] = high.T
            v_lo[cd, m:m + tile] = low.T

    for chunk in range(CHUNKS):
        start_collect(chunk)
    for chunk in range(CHUNKS):
        forward_collect(chunk)
    ahead = None
    for da in GROUPS:
        for chunk in range(CHUNKS):
            exchange(chunk, da)
            if ahead:
                multiply(*ahead)
            ahead = (chunk, da)
    multiply(*ahead)
    for chunk in range(CHUNKS):
        add_first(chunk)
    for chunk in range(CHUNKS):
        add_second(chunk)

    for chunk in range(CHUNKS):
        for da in range(SIDE):
            for db in range(SIDE):
                for flip in range(2):
                    if (da, db, flip) != (0, 0, 0):
                        spread(chunk, da, db, flip).wait_send()
                if db:
                    collect_b(chunk, da, db).wait_send()
                share(chunk, da, db).wait_send()
        for d in SHIFTS:
            collect_a(chunk, d).wait_send()
            for part in range(2):
                first_sum(chunk, part, d).wait_send()
                second_sum(chunk, part, d).wait_send()


def per_device(t2_stored, v_slab, block_source, r_in):
    ab, cd = v_slab.shape
    blocks = block_source.shape[0]
    stored = t2_stored.shape[1] // BLK
    owned = cd // BLK
    tiles = t2_stored.reshape(-1, ROWS, stored, BLK).transpose(0, 2, 1, 3)
    tiles = tiles.reshape(SLABS, CHUNKS, 2, stored, ROWS, BLK)
    group = SIDE * ROWS
    f32, bf16 = jnp.float32, jnp.bfloat16
    dma = pltpu.SemaphoreType.DMA
    ladder = pl.pallas_call(
        kernel,
        out_shape=jax.ShapeDtypeStruct(r_in.shape, f32),
        in_specs=[
            pl.BlockSpec(memory_space=pltpu.SMEM),
            pl.BlockSpec(memory_space=pl.ANY),
            pl.BlockSpec(memory_space=pl.ANY),
        ],
        out_specs=pl.BlockSpec(memory_space=pltpu.VMEM),
        scratch_shapes=[
            pltpu.VMEM((ab, cd), f32),
            pltpu.VMEM((cd, ab), bf16),
            pltpu.VMEM((cd, ab), bf16),
            pltpu.VMEM((blocks, ROWS, BLK), f32),
            pltpu.VMEM((blocks, ROWS, BLK), f32),
            pltpu.VMEM((CHUNKS, SIDE - 1, SIDE, ROWS, cd), f32),
            pltpu.VMEM((CHUNKS, SIDE, SIDE, ROWS, cd), f32),
            pltpu.VMEM((CHUNKS, 2, SIDE, SIDE, ROWS, cd), f32),
            pltpu.VMEM((4 * group, cd), bf16),
            pltpu.VMEM((CHUNKS, 2, SIDE, group, ab), f32),
            pltpu.VMEM((CHUNKS, 2, SIDE - 1, group, ab), f32),
            pltpu.VMEM((CHUNKS, 2, group, ab), f32),
            pltpu.VMEM((CHUNKS, 2, SIDE - 1, ROWS, ab), f32),
            dma,
            dma((CHUNKS, 2 * SIDE)),
            dma((CHUNKS, 2 * SLABS)),
            dma((CHUNKS, 2 * SLABS)),
            dma((CHUNKS, SIDE - 1)),
            dma((CHUNKS, SIDE - 1)),
            dma((CHUNKS, SIDE, SIDE - 1)),
            dma((CHUNKS, SIDE, SIDE - 1)),
            dma((CHUNKS, SIDE, SIDE)),
            dma((CHUNKS, SIDE, SIDE)),
            dma((CHUNKS, 2, SIDE - 1)),
            dma((CHUNKS, 2, SIDE - 1)),
            dma((CHUNKS, 2, SIDE - 1)),
            dma((CHUNKS, 2, SIDE - 1)),
        ],
        compiler_params=pltpu.CompilerParams(
            collective_id=1, has_side_effects=True, vmem_limit_bytes=60 * 1024 * 1024
        ),
        name="ladder",
    )(block_source, tiles, v_slab)
    return r_in + ladder


def solution(mesh):
    in_specs = (P("row", ("slab", "rep")), P("rep", "slab"), P(), P(("row", "slab"), "rep"))
    out_specs = P(("row", "slab"), "rep")
    return jax.shard_map(
        per_device, mesh=mesh, in_specs=in_specs, out_specs=out_specs, check_vma=False
    )
```

time: 298 us -> 92.5 us (0.31)
  waiting for transfers between devices: 114 us -> 0 us
  blocking collectives: 102 us -> 0 us
  Pallas kernels: 0 us -> 89.8 us
  local copies, waits for them, and re-layouts: 28.2 us -> 0.01 us
  matrix products: 28 us -> 0 us
  between operations: 13.5 us -> 0.02 us
  other arithmetic: 11.5 us -> 1.55 us
    all_to_all x1 -> x0, blocking collectives: 102 us -> none  [per_device(): lax.all_to_all(outgoing, 'slab', split_axis=1, concat_axis=1, tiled=True)]
    pallas_call x0 -> x1, Pallas kernels: none -> 89.8 us  [per_device(): pl.pallas_call(kernel, out_shape=jax.ShapeDtypeStruct(r_in.shape, f32), i...]
    reduce_scatter x1 -> x0, waiting for transfers between devices: 77.7 us -> none  [per_device(): lax.psum_scatter(partial_value, 'slab', scatter_dimension=0, tiled=True)]
    all_gather x1 -> x0, waiting for transfers between devices: 36.1 us -> none  [per_device(): copies = lax.all_gather(arrived, 'rep', axis=1, tiled=True)]
    dot_general x1 -> x0, matrix products: 28 us -> none  [per_device(): lax.dot_general(ordered, v_slab, (((1,), (1,)), ((), ())), precision=lax....]
    gather x7 -> x0, local copies, waits for them, and re-layouts: 22 us -> none  [the longest x2 14.9 us: per_device(): jnp.take(copies.reshape(row_count, -1, BLK), slot_ids, axis=1)]
    select_n x9 -> x0, other arithmetic: 8.43 us -> none  [the longest x1 5.17 us: per_device(): jnp.where(filled.reshape(1, -1, 1), picked, 0.0)]
    unnamed x5 -> x2, local copies, waits for them, and re-layouts: 3.63 us -> 0.01 us
  transfers between devices with their start and end apart: 2 -> 0, of which waited for: 2 -> 0; matrix products, arithmetic and copies ran while one was open for 1% -> 0% of each run, Pallas kernels for 0% -> 0%
where the time goes in v3:
time: 92.5 us; the launch traced here: 91.4 us
  Pallas kernels  89.8 us (97%)
  other arithmetic  1.55 us (2%)
    pallas_call x1, Pallas kernels, per_device(): pl.pallas_call(kernel, out_shape=jax.ShapeDtypeStruct(r_in.shape, f32), i...  89.8 us

profile of v3, /device:TPU:1, one launch (start us, length us, event | category | flops | bytes accessed | tf_op | source)
XLA Modules:
  0.0 91.4 jit_solution(9777085258406909561)
XLA Ops:
  0.0 0.0 copy-start
  0.0 89.8 %ladder.1 = f32[32,768]{1,0:T(8,128)} custom-call(s32[320]{0:T(512)} %source_ref.1, f32[16,2,2,10,8,128]{5,4,3,2,1,0:T(8,128)} %bitcast.5, f32[768,2560]{1,0:T(8,128)} %v_ref.1), custom_call_target="tpu_custom_call" | custom-call | tf_op jit(solution)/shard_map/ladder/pallas_call | solution.py:271
  89.8 0.0 copy-done
  89.8 1.5 %add.3 = f32[32,768]{1,0:T(8,128)} add(f32[32,768]{1,0:T(8,128)S(1)} %copy-done, f32[32,768]{1,0:T(8,128)} %ladder.1) | non-fusion elementwise | flops 24576 | bytes 294912 | tf_op jit(solution)/shard_map/add | solution.py:314
Async XLA Ops:
  0.0 89.8 %copy-start = (f32[32,768]{1,0:T(8,128)S(1)}, f32[32,768]{1,0:T(8,128)}, u32[]{:S(2)}) copy-start(f32[32,768]{1,0:T(8,128)} %param.7) | copy-start | bytes 294916

commit v4 on v3

--- a/solution.py
+++ b/solution.py
@@ -15,6 +15,7 @@
 
 SHIFTS = (2, 1, 3)
 ARRIVALS = (2, 1, 3)
+NEXT = (1, 3)
 SPREAD = sorted(
     [(da, db) for da in range(SIDE) for db in range(SIDE)],
     key=lambda d: -sum(min(n, SIDE - n) for n in d),
@@ -25,9 +26,9 @@
 def kernel(
     source_ref, t2_ref, v_ref, out_ref,
     v_raw, v_hi, v_lo, part_a, part_b, send_buf, relay2, whole, split,
-    ladder, level1, summed, level2,
+    ladder, folded, level1, summed, level2,
     v_sem, own_sem, send1, recv1, send3, recv3, send4, recv4,
-    send5, recv5, send6, recv6, send7, recv7,
+    send5, recv5, send6, recv6, send7, recv7, send8, recv8,
 ):
     row = lax.axis_index("row")
     slab = lax.axis_index("slab")
@@ -35,17 +36,22 @@
     x, y = slab // SIDE, slab % SIDE
     a = x + core * (y - x)
     b = y + core * (x - y)
+    a_step = SIDE - core * (SIDE - 1)
+    b_step = 1 + core * (SIDE - 1)
+    to_a = [(a + d) & (SIDE - 1) for d in range(SIDE)]
+    to_b = [(b + d) & (SIDE - 1) for d in range(SIDE)]
+    a_term = [n * a_step for n in to_a]
+    b_term = [n * b_step for n in to_b]
+    b_all = [n * b_step for n in range(SIDE)]
+    other = 1 - core
     stored = t2_ref.shape[3]
     owned = v_ref.shape[1] // BLK
     group = SIDE * ROWS
+    half = group // 2
     parts = (part_a, part_b)
 
-    def slab_at(aa, bb):
-        xx, yy = aa + core * (bb - aa), bb + core * (aa - bb)
-        return xx * SIDE + yy
-
     def device(da, db, flip=0):
-        return (row, slab_at((a + da + SIDE) % SIDE, (b + db + SIDE) % SIDE), (core + flip) % 2)
+        return (row, a_term[da % SIDE] + b_term[db % SIDE], other if flip else core)
 
     def remote(src, dst, send_sem, recv_sem, da, db, flip=0):
         return pltpu.make_async_remote_copy(
@@ -58,8 +64,7 @@
         )
 
     def spread(chunk, da, db, flip):
-        to_slab = slab_at((a + da) % SIDE, (b + db) % SIDE)
-        src = t2_ref.at[to_slab, chunk, (core + flip) % 2]
+        src = t2_ref.at[a_term[da] + b_term[db], chunk, other if flip else core]
         dst = parts[chunk].at[pl.ds((slab * 2 + core) * stored, stored)]
         if (da, db, flip) == (0, 0, 0):
             return pltpu.make_async_copy(src, dst, own_sem.at[chunk, 0])
@@ -68,8 +73,9 @@
 
     def spread_arrival(chunk, da, db, flip):
         ea, eb = (db, da) if flip else (da, db)
-        from_slab = slab_at((a - ea + SIDE) % SIDE, (b - eb + SIDE) % SIDE)
-        here = parts[chunk].at[pl.ds((from_slab * 2 + (core + flip) % 2) * stored, stored)]
+        from_slab = a_term[-ea % SIDE] + b_term[-eb % SIDE]
+        holder = from_slab * 2 + (other if flip else core)
+        here = parts[chunk].at[pl.ds(holder * stored, stored)]
         n = (da * SIDE + db) * 2 + flip
         return remote(here, here, send1.at[chunk, n], recv1.at[chunk, n], da, db, flip)
 
@@ -84,7 +90,7 @@
         )
 
     def collect_b(chunk, da, db):
-        src = relay2.at[chunk, (b + db) % SIDE, da]
+        src = relay2.at[chunk, to_b[db], da]
         dst = whole.at[chunk, 0, da, db]
         if db == 0:
             return pltpu.make_async_copy(src, dst, own_sem.at[chunk, SIDE + da])
@@ -96,12 +102,23 @@
         dst = whole.at[chunk, 1, da, db]
         return remote(src, dst, send5.at[chunk, da, db], recv5.at[chunk, da, db], 0, 0, 1)
 
+    def fold(chunk, part, d):
+        n = d // 2
+        return remote(
+            ladder.at[chunk, part, 2, pl.ds(n * half, half)],
+            folded.at[chunk, part, n],
+            send8.at[chunk, part, n],
+            recv8.at[chunk, part, n],
+            *((-d, 0), (0, -d))[part],
+        )
+
     def first_sum(chunk, part, d):
+        n = d // 2
         return remote(
             ladder.at[chunk, part, d],
-            level1.at[chunk, part, d - 1],
-            send6.at[chunk, part, d - 1],
-            recv6.at[chunk, part, d - 1],
+            level1.at[chunk, part, n],
+            send6.at[chunk, part, n],
+            recv6.at[chunk, part, n],
             *((-d, 0), (0, -d))[part],
         )
 
@@ -132,15 +149,15 @@
                 else:
                     spread_arrival(chunk, da, db, flip).wait_recv()
         for da in SHIFTS + (0,):
-            for to_b in range(SIDE):
-                first = slab_at((a + da) % SIDE, to_b) * owned
+            for its_b in range(SIDE):
+                first = (a_term[da] + b_all[its_b]) * owned
                 for k in range(owned):
                     piece = parts[chunk][source_ref[first + k]]
                     cols = slice(k * BLK, (k + 1) * BLK)
                     if da == 0:
-                        relay2[chunk, to_b, 0, :, cols] = piece
+                        relay2[chunk, its_b, 0, :, cols] = piece
                     else:
-                        send_buf[chunk, da - 1, to_b, :, cols] = piece
+                        send_buf[chunk, da - 1, its_b, :, cols] = piece
             if da:
                 collect_a(chunk, da).start()
         forward_blocks(chunk, 0)
@@ -172,17 +189,30 @@
         )
         total = both[0:2 * group] + (both[2 * group:] + low)
         for part in range(2):
-            ladder[chunk, part, da] = total[part * group:(part + 1) * group]
-            if da:
+            at = part * group
+            if da in NEXT:
+                fold(chunk, part, da).wait_recv()
+                n = da // 2
+                near = slice(n * half, (n + 1) * half)
+                far = slice((1 - n) * half, (2 - n) * half)
+                ladder[chunk, part, da, near] = (
+                    total[at + n * half:at + (n + 1) * half] + folded[chunk, part, n]
+                )
+                ladder[chunk, part, da, far] = total[at + (1 - n) * half:at + (2 - n) * half]
                 first_sum(chunk, part, da).start()
+            else:
+                ladder[chunk, part, da] = total[at:at + group]
+                if da:
+                    for d in NEXT:
+                        fold(chunk, part, d).start()
 
     def add_first(chunk):
         for part in range(2):
-            for d in ARRIVALS:
+            for d in NEXT:
                 first_sum(chunk, part, d).wait_recv()
-            summed[chunk, part] = (ladder[chunk, part, 0] + level1[chunk, part, 0]) + (
-                level1[chunk, part, 1] + level1[chunk, part, 2]
-            )
+            summed[chunk, part] = (
+                ladder[chunk, part, 0] + level1[chunk, part, 0]
+            ) + level1[chunk, part, 1]
             for d in SHIFTS:
                 second_sum(chunk, part, d).start()
 
@@ -191,7 +221,7 @@
             for d in SHIFTS:
                 second_sum(chunk, part, d).wait_recv()
             at = pl.ds(
-                pl.multiple_of((chunk * 2 + (core + part) % 2) * ROWS, ROWS), ROWS
+                pl.multiple_of((chunk * 2 + (other if part else core)) * ROWS, ROWS), ROWS
             )
             out_ref[at, :] = (summed[chunk, part, 0:ROWS, :] + level2[chunk, part, 0]) + (
                 level2[chunk, part, 1] + level2[chunk, part, 2]
@@ -254,8 +284,10 @@
         for d in SHIFTS:
             collect_a(chunk, d).wait_send()
             for part in range(2):
-                first_sum(chunk, part, d).wait_send()
                 second_sum(chunk, part, d).wait_send()
+                if d in NEXT:
+                    first_sum(chunk, part, d).wait_send()
+                    fold(chunk, part, d).wait_send()
 
 
 def per_device(t2_stored, v_slab, block_source, r_in):
@@ -288,7 +320,8 @@
             pltpu.VMEM((CHUNKS, 2, SIDE, SIDE, ROWS, cd), f32),
             pltpu.VMEM((4 * group, cd), bf16),
             pltpu.VMEM((CHUNKS, 2, SIDE, group, ab), f32),
-            pltpu.VMEM((CHUNKS, 2, SIDE - 1, group, ab), f32),
+            pltpu.VMEM((CHUNKS, 2, 2, group // 2, ab), f32),
+            pltpu.VMEM((CHUNKS, 2, 2, group, ab), f32),
             pltpu.VMEM((CHUNKS, 2, group, ab), f32),
             pltpu.VMEM((CHUNKS, 2, SIDE - 1, ROWS, ab), f32),
             dma,
@@ -301,10 +334,12 @@
             dma((CHUNKS, SIDE, SIDE - 1)),
             dma((CHUNKS, SIDE, SIDE)),
             dma((CHUNKS, SIDE, SIDE)),
+            dma((CHUNKS, 2, 2)),
+            dma((CHUNKS, 2, 2)),
             dma((CHUNKS, 2, SIDE - 1)),
             dma((CHUNKS, 2, SIDE - 1)),
-            dma((CHUNKS, 2, SIDE - 1)),
-            dma((CHUNKS, 2, SIDE - 1)),
+            dma((CHUNKS, 2, 2)),
+            dma((CHUNKS, 2, 2)),
         ],
         compiler_params=pltpu.CompilerParams(
             collective_id=1, has_side_effects=True, vmem_limit_bytes=60 * 1024 * 1024

time: 92.5 us -> 90.6 us (0.979); the launches traced: 91.4 us -> 90.5 us
  no operation moved by 1% of the time
where the time goes in v4:
time: 90.6 us; the launch traced here: 90.5 us
  Pallas kernels  88.9 us (98%)
  other arithmetic  1.55 us (2%)
    pallas_call x1, Pallas kernels, per_device(): pl.pallas_call(kernel, out_shape=jax.ShapeDtypeStruct(r_in.shape, f32), i...  88.9 us

profile of v4, /device:TPU:1, one launch (start us, length us, event | category | flops | bytes accessed | tf_op | source)
XLA Modules:
  0.0 90.5 jit_solution(18088619432585559397)
XLA Ops:
  0.0 0.0 copy-start
  0.0 88.9 %ladder.1 = f32[32,768]{1,0:T(8,128)} custom-call(s32[320]{0:T(512)} %source_ref.1, f32[16,2,2,10,8,128]{5,4,3,2,1,0:T(8,128)} %bitcast.5, f32[768,2560]{1,0:T(8,128)} %v_ref.1), custom_call_target="tpu_custom_call" | custom-call | tf_op jit(solution)/shard_map/ladder/pallas_call | solution.py:303
  88.9 0.0 copy-done
  88.9 1.5 %add.3 = f32[32,768]{1,0:T(8,128)} add(f32[32,768]{1,0:T(8,128)S(1)} %copy-done, f32[32,768]{1,0:T(8,128)} %ladder.1) | non-fusion elementwise | flops 24576 | bytes 294912 | tf_op jit(solution)/shard_map/add | solution.py:349
Async XLA Ops:
  0.0 88.9 %copy-start = (f32[32,768]{1,0:T(8,128)S(1)}, f32[32,768]{1,0:T(8,128)}, u32[]{:S(2)}) copy-start(f32[32,768]{1,0:T(8,128)} %param.7) | copy-start | bytes 294916

commit v5 on v4

--- a/solution.py
+++ b/solution.py
@@ -25,9 +25,9 @@
 
 def kernel(
     source_ref, t2_ref, v_ref, out_ref,
-    v_raw, v_hi, v_lo, part_a, part_b, send_buf, relay2, whole, split,
+    v_raw, v_hi, v_lo, swapped, part_a, part_b, send_buf, relay2, whole, split,
     ladder, folded, level1, summed, level2,
-    v_sem, own_sem, send1, recv1, send3, recv3, send4, recv4,
+    v_sem, swap_sem, own_sem, send1, recv1, send3, recv3, send4, recv4,
     send5, recv5, send6, recv6, send7, recv7, send8, recv8,
 ):
     row = lax.axis_index("row")
@@ -63,21 +63,35 @@
             device_id_type=MESH,
         )
 
+    def swap(chunk):
+        return remote(
+            t2_ref.at[:, chunk, other],
+            swapped.at[chunk],
+            swap_sem.at[2 * chunk],
+            swap_sem.at[2 * chunk + 1],
+            0,
+            0,
+            1,
+        )
+
     def spread(chunk, da, db, flip):
-        src = t2_ref.at[a_term[da] + b_term[db], chunk, other if flip else core]
-        dst = parts[chunk].at[pl.ds((slab * 2 + core) * stored, stored)]
-        if (da, db, flip) == (0, 0, 0):
-            return pltpu.make_async_copy(src, dst, own_sem.at[chunk, 0])
+        to_slab = a_term[da] + b_term[db]
+        if flip:
+            src = swapped.at[chunk, to_slab]
+        else:
+            src = t2_ref.at[to_slab, chunk, core]
+        holder = slab * 2 + (other if flip else core)
+        dst = parts[chunk].at[pl.ds(holder * stored, stored)]
+        if (da, db) == (0, 0):
+            return pltpu.make_async_copy(src, dst, swap_sem.at[4 + 2 * chunk + flip])
         n = (da * SIDE + db) * 2 + flip
-        return remote(src, dst, send1.at[chunk, n], recv1.at[chunk, n], da, db, flip)
+        return remote(src, dst, send1.at[chunk, n], recv1.at[chunk, n], da, db)
 
     def spread_arrival(chunk, da, db, flip):
-        ea, eb = (db, da) if flip else (da, db)
-        from_slab = a_term[-ea % SIDE] + b_term[-eb % SIDE]
-        holder = from_slab * 2 + (other if flip else core)
+        holder = (a_term[-da % SIDE] + b_term[-db % SIDE]) * 2 + (other if flip else core)
         here = parts[chunk].at[pl.ds(holder * stored, stored)]
         n = (da * SIDE + db) * 2 + flip
-        return remote(here, here, send1.at[chunk, n], recv1.at[chunk, n], da, db, flip)
+        return remote(here, here, send1.at[chunk, n], recv1.at[chunk, n], da, db)
 
     def collect_a(chunk, da):
         return remote(
@@ -131,10 +145,9 @@
             *((0, -d), (-d, 0))[part],
         )
 
-    def start_spread(chunk):
+    def start_spread(chunk, flip):
         for da, db in SPREAD:
-            for flip in range(2):
-                spread(chunk, da, db, flip).start()
+            spread(chunk, da, db, flip).start()
 
     def forward_blocks(chunk, da):
         for db in SHIFTS + (0,):
@@ -144,8 +157,8 @@
     def start_collect(chunk):
         for da, db in SPREAD:
             for flip in range(2):
-                if (da, db, flip) == (0, 0, 0):
-                    spread(chunk, 0, 0, 0).wait()
+                if (da, db) == (0, 0):
+                    spread(chunk, 0, 0, flip).wait()
                 else:
                     spread_arrival(chunk, da, db, flip).wait_recv()
         for da in SHIFTS + (0,):
@@ -231,16 +244,17 @@
     v_copy.start()
 
     barrier = pltpu.get_barrier_semaphore()
-    for da, db in SPREAD:
-        for flip in range(2):
-            if (da, db, flip) != (0, 0, 0):
-                pl.semaphore_signal(
-                    barrier, inc=1, device_id=device(da, db, flip), device_id_type=MESH
-                )
-    pl.semaphore_wait(barrier, 2 * SLABS - 1)
-
-    start_spread(0)
-    start_spread(1)
+    greeted = [(da, db, 0) for da, db in SPREAD[:-1]] + [(0, 0, 1)]
+    for da, db, flip in greeted:
+        pl.semaphore_signal(barrier, inc=1, device_id=device(da, db, flip), device_id_type=MESH)
+    pl.semaphore_wait(barrier, len(greeted))
+
+    for chunk in range(CHUNKS):
+        swap(chunk).start()
+    for chunk in range(CHUNKS):
+        start_spread(chunk, 0)
+        swap(chunk).wait()
+        start_spread(chunk, 1)
 
     v_copy.wait()
     tile = 256
@@ -276,7 +290,7 @@
         for da in range(SIDE):
             for db in range(SIDE):
                 for flip in range(2):
-                    if (da, db, flip) != (0, 0, 0):
+                    if (da, db) != (0, 0):
                         spread(chunk, da, db, flip).wait_send()
                 if db:
                     collect_b(chunk, da, db).wait_send()
@@ -313,6 +327,7 @@
             pltpu.VMEM((ab, cd), f32),
             pltpu.VMEM((cd, ab), bf16),
             pltpu.VMEM((cd, ab), bf16),
+            pltpu.VMEM((CHUNKS, SLABS, stored, ROWS, BLK), f32),
             pltpu.VMEM((blocks, ROWS, BLK), f32),
             pltpu.VMEM((blocks, ROWS, BLK), f32),
             pltpu.VMEM((CHUNKS, SIDE - 1, SIDE, ROWS, cd), f32),
@@ -325,6 +340,7 @@
             pltpu.VMEM((CHUNKS, 2, group, ab), f32),
             pltpu.VMEM((CHUNKS, 2, SIDE - 1, ROWS, ab), f32),
             dma,
+            dma((4 * CHUNKS,)),
             dma((CHUNKS, 2 * SIDE)),
             dma((CHUNKS, 2 * SLABS)),
             dma((CHUNKS, 2 * SLABS)),

time: 90.6 us -> 87.3 us (0.964)
  Pallas kernels: 88.9 us -> 85.6 us
    pallas_call x1, Pallas kernels: 88.9 us -> 85.6 us  [per_device(): pl.pallas_call(kernel, out_shape=jax.ShapeDtypeStruct(r_in.shape, f32), i...]
where the time goes in v5:
time: 87.3 us; the launch traced here: 87.2 us
  Pallas kernels  85.6 us (98%)
  other arithmetic  1.55 us (2%)
    pallas_call x1, Pallas kernels, per_device(): pl.pallas_call(kernel, out_shape=jax.ShapeDtypeStruct(r_in.shape, f32), i...  85.6 us

profile of v5, /device:TPU:1, one launch (start us, length us, event | category | flops | bytes accessed | tf_op | source)
XLA Modules:
  0.0 87.2 jit_solution(8891883057265837679)
XLA Ops:
  0.0 0.0 copy-start
  0.0 85.6 %ladder.1 = f32[32,768]{1,0:T(8,128)} custom-call(s32[320]{0:T(512)} %source_ref.1, f32[16,2,2,10,8,128]{5,4,3,2,1,0:T(8,128)} %bitcast.5, f32[768,2560]{1,0:T(8,128)} %v_ref.1), custom_call_target="tpu_custom_call" | custom-call | tf_op jit(solution)/shard_map/ladder/pallas_call | solution.py:317
  85.6 0.0 copy-done
  85.7 1.5 %add.3 = f32[32,768]{1,0:T(8,128)} add(f32[32,768]{1,0:T(8,128)S(1)} %copy-done, f32[32,768]{1,0:T(8,128)} %ladder.1) | non-fusion elementwise | flops 24576 | bytes 294912 | tf_op jit(solution)/shard_map/add | solution.py:365
Async XLA Ops:
  0.0 85.7 %copy-start = (f32[32,768]{1,0:T(8,128)S(1)}, f32[32,768]{1,0:T(8,128)}, u32[]{:S(2)}) copy-start(f32[32,768]{1,0:T(8,128)} %param.7) | copy-start | bytes 294916

commit v6 on v5

--- a/solution.py
+++ b/solution.py
@@ -273,14 +273,11 @@
         start_collect(chunk)
     for chunk in range(CHUNKS):
         forward_collect(chunk)
-    ahead = None
     for da in GROUPS:
         for chunk in range(CHUNKS):
             exchange(chunk, da)
-            if ahead:
-                multiply(*ahead)
-            ahead = (chunk, da)
-    multiply(*ahead)
+        for chunk in range(CHUNKS):
+            multiply(chunk, da)
     for chunk in range(CHUNKS):
         add_first(chunk)
     for chunk in range(CHUNKS):

time: 87.3 us -> 90.7 us (1.039)
  Pallas kernels: 85.6 us -> 89 us
    pallas_call x1, Pallas kernels: 85.6 us -> 89 us  [per_device(): pl.pallas_call(kernel, out_shape=jax.ShapeDtypeStruct(r_in.shape, f32), i...]
where the time goes in v6:
time: 90.7 us; the launch traced here: 90.6 us
  Pallas kernels  89 us (98%)
  other arithmetic  1.55 us (2%)
    pallas_call x1, Pallas kernels, per_device(): pl.pallas_call(kernel, out_shape=jax.ShapeDtypeStruct(r_in.shape, f32), i...  89 us

profile of v6, /device:TPU:1, one launch (start us, length us, event | category | flops | bytes accessed | tf_op | source)
XLA Modules:
  0.0 90.6 jit_solution(14561212701427034261)
XLA Ops:
  0.0 0.0 copy-start
  0.0 89.0 %ladder.1 = f32[32,768]{1,0:T(8,128)} custom-call(s32[320]{0:T(512)} %source_ref.1, f32[16,2,2,10,8,128]{5,4,3,2,1,0:T(8,128)} %bitcast.5, f32[768,2560]{1,0:T(8,128)} %v_ref.1), custom_call_target="tpu_custom_call" | custom-call | tf_op jit(solution)/shard_map/ladder/pallas_call | solution.py:314
  89.0 0.0 copy-done
  89.0 1.5 %add.3 = f32[32,768]{1,0:T(8,128)} add(f32[32,768]{1,0:T(8,128)S(1)} %copy-done, f32[32,768]{1,0:T(8,128)} %ladder.1) | non-fusion elementwise | flops 24576 | bytes 294912 | tf_op jit(solution)/shard_map/add | solution.py:362
Async XLA Ops:
  0.0 89.0 %copy-start = (f32[32,768]{1,0:T(8,128)S(1)}, f32[32,768]{1,0:T(8,128)}, u32[]{:S(2)}) copy-start(f32[32,768]{1,0:T(8,128)} %param.7) | copy-start | bytes 294916
